TPU v7x, 256 devices: a whole 4x4x8 slice. The times are simulated.
256 devices in a mesh: section: 2 (over core), seq: 8 (over z), chan: 16 (over y, x).
Axes of the slice: x: 4, y: 4, z: 8, core: 2. Of those that a mesh axis runs over, the one named last changes fastest.
Arguments:
- inputs: bfloat16 [2, 512, 4096], P(None, 'seq', 'chan'), may hold values from -8 to 8
- out_grad: bfloat16 [2, 512, 4096], P(None, 'seq', 'chan'), may hold values from -0.5 to 0.5
- short_filters: float32 [2, 3, 7, 4096], P('section', None, None, 'chan'), may hold values from -2 to 2
- long_filters: float32 [2, 128, 4096], P('section', None, 'chan'), may hold values from -0.5 to 0.5
- skip_gain: float32 [2, 4096], P('section', 'chan'), may hold values from -1 to 1
- norm_gain: float32 [2, 4096], P('section', 'chan'), may hold values from 0.5 to 1.5
Outputs:
- param_grads: float32 [2, 151, 4096], P('section', None, 'chan')
All inputs are finite; a program needn't handle non-finite values.
Results may differ from a plain program's by a relative error of at most 0.012.
The roundings to bfloat16 on the way count: a program that leaves them out, or rounds other values in their place, can miss the bound.
Values may be sent and summed in bfloat16 or wider, within the bound.
No kernel may reach another device: no remote copies, remote signals or barrier semaphores. Data moves between devices by JAX's collectives and lax.ppermute only.
A program may use at most 64 MiB of HBM per device.

v0:
```python
import functools

import jax
import jax.numpy as jnp
from jax import lax
from jax.experimental import pallas as pl
from jax.experimental.pallas import tpu as pltpu
from jax.sharding import PartitionSpec as P

EPSILON = 1e-06
SHARDS = 8
ROWS = 64
LANES = 128
KS = 7
KL = 128
PARAMS = 152
UNROLLED = 3
PARTS = 9
SHORT_AT, SKIP_AT, GAIN_AT, TAPS = 288, 309, 310, 312
QUARTER = ROWS // 4
SHORT_ROWS = 32
MESSAGE = SHORT_ROWS + 32
f32 = jnp.float32
bf16 = jnp.bfloat16


def rounded(a):
    return a.astype(bf16).astype(f32)


def later(a, count):
    sub = lax.broadcasted_iota(jnp.int32, a.shape, 1)
    return jnp.where(sub >= count, pltpu.roll(a, count, 1), 0.0)


def sooner(a, count):
    sub = lax.broadcasted_iota(jnp.int32, a.shape, 1)
    return jnp.where(sub < SHARDS - count, pltpu.roll(a, SHARDS - count, 1), 0.0)


def eye():
    shape = (LANES, LANES)
    return lax.broadcasted_iota(jnp.int32, shape, 0) == lax.broadcasted_iota(jnp.int32, shape, 1)


def send_sums(out_ref, chunk_of):
    diagonal = eye()
    rows = []
    for b in range(4):
        column = jnp.sum(chunk_of(b), axis=1, keepdims=True)
        rows.append(jnp.sum(jnp.where(diagonal, column, 0.0), axis=0, keepdims=True))
    whole = jnp.concatenate(rows, axis=0)
    out_ref[...] = jnp.broadcast_to(whole[None], out_ref.shape)


def column_of(row, diagonal):
    column = jnp.sum(jnp.where(diagonal, row, 0.0), axis=1, keepdims=True)
    return jnp.broadcast_to(column, (LANES, LANES)).reshape(16, SHARDS, LANES)


def sixteen_of(ref, b):
    if len(ref.shape) == 3:
        return ref[pl.ds(16 * b, 16)]
    at = pl.ds(pl.multiple_of(b * LANES, LANES), LANES)
    return ref[at, :].astype(f32).reshape(16, SHARDS, LANES)


def scale_and_norm(width, x_ref, sums_ref, taps, scale_ref, normed):
    total = jnp.sum(sums_ref[...], axis=0)
    scale_rows = lax.rsqrt(total * (1.0 / width) + EPSILON)
    diagonal = eye()
    gain = taps[GAIN_AT]
    for b in range(4):
        scale = column_of(scale_rows[b : b + 1], diagonal)
        scale_ref[pl.ds(16 * b, 16)] = scale
        normed[pl.ds(8 + 16 * b, 16)] = rounded(sixteen_of(x_ref, b) * scale * gain[None])
    normed[pl.ds(0, 8)] = later(normed[pl.ds(64, 8)], 1)
    return scale_rows


def forward(taps, normed, mixed, signals, results, q_ref, k_ref, v_ref, f_ref):
    @pl.loop(0, ROWS // 8)
    def _(b):
        near = normed[pl.ds(b * 8, 16)]
        streams = []
        for i in range(3):
            total = None
            for j in range(KS):
                term = taps[SHORT_AT + KS * i + j][None] * near[8 - j : 16 - j]
                total = term if total is None else total + term
            streams.append(total)
        at = pl.ds(b * 8, 8)
        q_ref[at] = streams[0]
        k_ref[at] = streams[1]
        v_ref[at] = streams[2]
        z = rounded(streams[1] * streams[2])
        mixed[pl.ds(128 + b * 8, 8)] = z
        mixed[pl.ds(64 + b * 8, 8)] = later(z, 1)
        mixed[pl.ds(b * 8, 8)] = later(z, 2)

    split(mixed, 1, signals, REVERSED, 6)
    convolve(taps, signals, results, True, 16)
    skip = taps[SKIP_AT][None]
    for half in range(2):
        at = pl.ds(32 * half, 32)
        f_ref[at] = skip * mixed[pl.ds(128 + 32 * half, 32)] + joined(results, REVERSED, 8 * half, 8)


def split(ref, start, signals, order, blocks):
    @pl.loop(0, blocks)
    def _(g):
        near = ref[pl.ds(start + 32 * g, 32)].reshape(8, 4, SHARDS, LANES)
        far = ref[pl.ds(start + 4 + 32 * g, 32)].reshape(8, 4, SHARDS, LANES)
        s = [near[:, 0], near[:, 1], near[:, 2], near[:, 3], far[:, 0], far[:, 1], far[:, 2]]
        one = (s[1], s[3], s[5])
        two = (s[0] - s[1], s[2] - s[3], s[4] - s[5])
        three = (s[2] - s[1], s[4] - s[3], s[6] - s[5])
        for t, (before, middle, after) in enumerate((one, two, three)):
            for p, part in enumerate((middle, before - middle, after - middle)):
                signals[order[3 * t + p], pl.ds(8 * g, 8)] = part


STRAIGHT = (0, 1, 2, 3, 4, 5, 6, 7, 8)
REVERSED = (0, 2, 1, 6, 8, 7, 3, 5, 4)


def convolve(taps, signals, results, backwards, count):
    @pl.loop(0, PARTS // UNROLLED)
    def _(several):
        for one in range(UNROLLED):
            u = several * UNROLLED + one
            total = jnp.zeros((count, SHARDS, LANES), f32)
            for g in range(2):
                z = signals[u, pl.ds(16 * g, count + 15)]
                w = taps[pl.ds(32 * u + 16 * (1 - g if backwards else g), 16)]
                for a in range(16):
                    total = total + w[15 - a if backwards else a][None] * z[a : a + count]
            results[u, pl.ds(0, count)] = total


def joined(results, order, start, count):
    even, odd = [], []
    for t in range(3):
        middle, first, last = (results[order[3 * t + p], pl.ds(start, count)] for p in range(3))
        even.append(middle + first)
        odd.append(middle + last)
    rows = [even[0] + even[1], even[0] + even[2], odd[0] + odd[1], odd[0] + odd[2]]
    return jnp.stack(rows, axis=1).reshape(4 * count, SHARDS, LANES)


def extend_after(ref, blocks):
    if blocks == 1:
        ref[pl.ds(64, 8)] = sooner(ref[pl.ds(0, 8)], 1)
        return

    @pl.loop(0, 8)
    def _(b):
        a = ref[pl.ds(b * 8, 8)]
        ref[pl.ds(64 + b * 8, 8)] = sooner(a, 1)
        ref[pl.ds(128 + b * 8, 8)] = sooner(a, 2)

    ref[pl.ds(192, 8)] = sooner(ref[pl.ds(0, 8)], 3)


def normed_cotangent(taps, streams, start):
    total = None
    for i in range(3):
        near = streams[i][pl.ds(start, 16)]
        for j in range(KS):
            term = taps[SHORT_AT + KS * i + j][None] * near[j : j + 8]
            total = term if total is None else total + term
    return total


def over_shards(a):
    return jnp.sum(a, axis=1)


def sums_of_rows(out_ref, streams, start, near, product, gain_term):
    rows = []
    for i in range(3):
        stream = streams[i][pl.ds(start, QUARTER)]
        for j in range(KS):
            rows.append(jnp.sum(stream * near[8 - j : 8 - j + QUARTER], axis=0))
    rows.append(jnp.sum(product, axis=0))
    rows.append(gain_term)
    while len(rows) < SHORT_ROWS:
        rows.append(jnp.zeros((SHARDS, LANES), f32))
    out_ref[pl.ds(0, SHORT_ROWS), :] = over_shards(jnp.stack(rows, axis=0))


def long_sums(out_ref, at, after, window):
    for half in range(2):
        sums = [None] * 16
        for b in range(ROWS // 16):
            d = after[pl.ds(b * 16, 16)]
            z = window[pl.ds(17 + 16 * (b - half), 31)]
            for a in range(16):
                term = jnp.sum(d * z[15 - a : 31 - a], axis=0)
                sums[a] = term if b == 0 else sums[a] + term
        out_ref[pl.ds(at + half * 16, 16), :] = over_shards(jnp.stack(sums, axis=0))


def flat(a):
    return a.reshape(ROWS * SHARDS, LANES).astype(bf16)


def rows_of(ref, b):
    at = pl.ds(pl.multiple_of(b * 64, 64), 64)
    return ref[at, :].astype(f32).reshape(8, SHARDS, LANES)


def window_before(own_ref, q, window):
    @pl.loop(0, 14)
    def _(b):
        block = 12 - 4 * q + b
        z = rows_of(own_ref, block % 8)
        back = block // 8
        window[pl.ds(8 * b, 8)] = jnp.where(back == 2, z, jnp.where(back == 1, later(z, 1), later(z, 2)))


def pack_kernel(x_ref, g_ref, out_ref, held, sems):
    mine = pl.ds(pl.multiple_of(lax.axis_index("section") * LANES, LANES), LANES)
    copies = [pltpu.make_async_copy(ref, held.at[part], sems.at[part]) for part, ref in enumerate((x_ref, g_ref))]
    for copy in copies:
        copy.start()
    for part, copy in enumerate(copies):
        copy.wait()
        for z in range(SHARDS):
            out_ref[z, pl.ds(part * ROWS, ROWS), :] = held[part, z % 2, :, mine]


def halves_kernel(short_hbm, long_hbm, skip_hbm, gain_hbm, own_ref, send_ref, short_ref, long_ref, skip_ref, gain_ref, sems):
    section = lax.axis_index("section")
    mine = pl.ds(pl.multiple_of(section * LANES, LANES), LANES)
    other = pl.ds(pl.multiple_of((1 - section) * LANES, LANES), LANES)
    pairs = ((short_hbm, short_ref), (long_hbm, long_ref), (skip_hbm, skip_ref), (gain_hbm, gain_ref))
    copies = [pltpu.make_async_copy(a, b, sems.at[k]) for k, (a, b) in enumerate(pairs)]
    for copy in copies:
        copy.start()
    for copy in copies:
        copy.wait()
    for ref, half in ((own_ref, mine), (send_ref, other)):
        ref[pl.ds(0, KL), :] = long_ref[0, :, half]
        for i in range(3):
            for j in range(KS):
                ref[pl.ds(KL + KS * i + j, 1), :] = short_ref[i, j, :, half]
        ref[pl.ds(KL + 3 * KS, 1), :] = skip_ref[:, half]
        ref[pl.ds(KL + 3 * KS + 1, 1), :] = gain_ref[:, half]
        ref[pl.ds(PARAMS - 1, 1), :] = jnp.zeros((1, LANES), f32)


def spread(own_ref, other_ref, layer, taps):
    mine = lax.axis_index("section") == layer

    def rows_at(g):
        at = pl.ds(pl.multiple_of(g * 8, 8), 8)
        rows = jnp.where(mine, own_ref[at, :], other_ref[at, :])
        return [jnp.broadcast_to(rows[k : k + 1], (8, LANES)) for k in range(8)]

    @pl.loop(0, KL // 8)
    def _(g):
        rows = rows_at(g)
        for half in range(2):
            a, b, c, d = rows[4 * half : 4 * half + 4]
            parts = (a + b + (c + d), a + b, c + d, a + c, a, c, b + d, b, d)
            for u, part in enumerate(parts):
                taps[32 * u + 2 * g + half] = part

    for g in range(3):
        for k, row in enumerate(rows_at(KL // 8 + g)):
            taps[SHORT_AT + 8 * g + k] = row


def spread_kernel(own_ref, other_ref, taps0, token_ref):
    spread(own_ref, other_ref, 0, taps0)
    token_ref[...] = jnp.zeros_like(token_ref)


def open_kernel(in_ref, token_ref, x_ref, g_ref, out_ref, wide):
    unpack(in_ref, 0, wide, x_ref)

    def chunk(b):
        x = x_ref[pl.ds(16 * b, 16)].reshape(LANES, LANES)
        return x * x

    send_sums(out_ref, chunk)
    unpack(in_ref, 1, wide, g_ref)


def unpack(in_ref, part, wide, ref):
    for z in range(SHARDS):
        wide[pl.ds(z * ROWS, ROWS), :] = in_ref[z, pl.ds(part * ROWS, ROWS), :].astype(f32)
    for v in range(ROWS):
        ref[v] = wide[pl.ds(v, SHARDS, stride=ROWS), :]


def first_kernel(
    width, x_ref, sums_ref, taps,
    x1_ref, q_ref, mixed_ref, normed_part, f_part, k_part, v_part, scaled_part, out_ref,
    mixed, normed, scale_ref, f_ref, k_ref, v_ref, signals, results
):
    scale_and_norm(width, x_ref, sums_ref, taps, scale_ref, normed)
    forward(taps, normed, mixed, signals, results, q_ref, k_ref, v_ref, f_ref)

    def chunk(b):
        at = pl.ds(16 * b, 16)
        x1 = rounded(x_ref[at] + q_ref[at] * f_ref[at])
        x1 = x1.reshape(LANES, LANES)
        x1_ref[pl.ds(LANES * b, LANES), :] = x1.astype(bf16)
        return x1 * x1

    send_sums(out_ref, chunk)
    mixed_ref[...] = flat(mixed[pl.ds(128, ROWS)])
    start = (lax.axis_index("seq") // 2) * QUARTER
    for ref, part in ((f_ref, f_part), (k_ref, k_part), (v_ref, v_part)):
        extend_after(ref, 1)
        part[...] = ref[pl.ds(start, QUARTER + 8)]
    normed_part[...] = normed[pl.ds(start, QUARTER + 8)]
    at = pl.ds(start, QUARTER)
    scaled_part[...] = x_ref[at] * scale_ref[at]


def second_kernel(
    width, x_ref, g_ref, sums_ref, own_ref, other_ref,
    base_ref, cubes_ref, after_ref, mixed_ref, grads_ref, out_ref,
    normed, mixed, after, sq, sk, sv, q_ref, k_ref, v_ref, f_ref, scale_ref, d_ref, signals, results, taps, parts, sem
):
    spread(own_ref, other_ref, 1, taps)
    scale_rows = scale_and_norm(width, x_ref, sums_ref, taps, scale_ref, normed)
    cubes_ref[...] = scale_rows * scale_rows * scale_rows * (1.0 / width)
    forward(taps, normed, mixed, signals, results, q_ref, k_ref, v_ref, f_ref)

    @pl.loop(0, ROWS // 8)
    def _(b):
        at = pl.ds(b * 8, 8)
        e = g_ref[at]
        sq[at] = rounded(e * f_ref[at])
        d_filtered = rounded(e * q_ref[at])
        after[at] = d_filtered

    extend_after(after, 17)

    split(after, 0, signals, STRAIGHT, 6)
    convolve(taps, signals, results, False, 16)
    skip = taps[SKIP_AT][None]
    for half in range(2):
        at = pl.ds(32 * half, 32)
        d_mixed = skip * after[at] + joined(results, STRAIGHT, 8 * half, 8)
        sk[at] = rounded(d_mixed * v_ref[at])
        sv[at] = rounded(d_mixed * k_ref[at])

    for ref in (sq, sk, sv):
        extend_after(ref, 1)

    gain = taps[GAIN_AT][None]

    @pl.loop(0, ROWS // 8)
    def _(b):
        at = pl.ds(b * 8, 8)
        d_normed = normed_cotangent(taps, (sq, sk, sv), b * 8)
        k_ref[at] = d_normed
        d_ref[at] = gain * d_normed * rows_of(x_ref, b)

    def chunk(b):
        return d_ref[pl.ds(16 * b, 16)].reshape(LANES, LANES)

    send_sums(parts, chunk)
    copy = pltpu.make_async_copy(parts, out_ref, sem)
    copy.start()

    @pl.loop(0, ROWS // 8)
    def _(b):
        at = pl.ds(b * 8, 8)
        base_ref[at] = g_ref[at] + scale_ref[at] * gain * k_ref[at]

    mixed_ref[...] = flat(mixed[pl.ds(128, ROWS)])
    after_ref[...] = flat(after[pl.ds(0, ROWS)])
    start = (lax.axis_index("seq") // 2) * QUARTER
    at = pl.ds(start, QUARTER)
    sums_of_rows(
        grads_ref, (sq, sk, sv), start, normed[pl.ds(start, QUARTER + 8)],
        after[at] * mixed[pl.ds(128 + start, QUARTER)],
        jnp.sum(k_ref[at] * sixteen_of(x_ref, start // QUARTER) * scale_ref[at], axis=0),
    )
    copy.wait()


def aside_kernel(after_ref, mixed1_ref, mixed0_ref, own_ref, other_ref, grads_ref, window0, taps, window1, after):
    q = lax.axis_index("seq") // 2
    window_before(mixed1_ref, q, window1)

    @pl.loop(0, ROWS // 8)
    def _(b):
        after[pl.ds(b * 8, 8)] = rows_of(after_ref, b)

    long_sums(grads_ref, 0, after, window1)
    window_before(mixed0_ref, q, window0)
    spread(own_ref, other_ref, 0, taps)


def third_kernel(
    base_ref, x1_ref, cubes_ref, sums_ref, taps, window, scaled_part, normed_part, mixed_ref, q_ref, f_part, k_part, v_part,
    short1_ref, long1_ref, out_ref, after, errors, sq, sk, sv, grads, signals, results
):
    q = lax.axis_index("seq") // 2
    total = jnp.sum(sums_ref[...], axis=0) * cubes_ref[...]
    diagonal = eye()
    for b in range(4):
        at = pl.ds(16 * b, 16)
        e = rounded(base_ref[at] - sixteen_of(x1_ref, b) * column_of(total[b : b + 1], diagonal))
        errors[at] = e
        after[at] = rounded(e * q_ref[at])
    extend_after(after, 17)
    extend_after(errors, 1)
    start = q * QUARTER

    split(after, start, signals, STRAIGHT, 5)
    convolve(taps, signals, results, False, 6)
    at = pl.ds(start, QUARTER + 8)
    d_mixed = taps[SKIP_AT][None] * after[at] + joined(results, STRAIGHT, 0, 6)
    sq[at] = rounded(errors[at] * f_part[...])
    sk[at] = rounded(d_mixed * v_part[...])
    sv[at] = rounded(d_mixed * k_part[...])

    gain_term = jnp.zeros((SHARDS, LANES), f32)
    for b in range(2):
        d_normed = normed_cotangent(taps, (sq, sk, sv), start + 8 * b)
        gain_term = gain_term + jnp.sum(d_normed * scaled_part[pl.ds(8 * b, 8)], axis=0)
    product = after[pl.ds(start, QUARTER)] * sixteen_of(mixed_ref, q)
    sums_of_rows(grads, (sq, sk, sv), start, normed_part[...], product, gain_term)
    long_sums(grads, SHORT_ROWS, after, window)
    message0 = grads[...].astype(bf16)
    message1 = jnp.concatenate([short1_ref[...], long1_ref[...]], axis=0).astype(bf16)
    for z in range(SHARDS):
        out_ref[z] = message0
        out_ref[SHARDS + z] = message1


def close_kernel(in_ref, out_ref, whole, sems):
    sums = [None, None]
    copies = []

    def leave(first, count):
        at = pl.ds(first, count)
        copies.append(pltpu.make_async_copy(whole.at[at], out_ref.at[at], sems.at[len(copies)]))
        copies[-1].start()

    for q in range(4):
        for half in range(2):
            lanes = pl.ds(half * LANES, LANES)
            pair = in_ref[half * SHARDS + 2 * q].astype(f32) + in_ref[half * SHARDS + 2 * q + 1].astype(f32)
            whole[pl.ds(3 * KS + 32 * q, 32), 0, lanes] = pair[SHORT_ROWS:]
            sums[half] = pair[:SHORT_ROWS] if q == 0 else sums[half] + pair[:SHORT_ROWS]
        leave(3 * KS + 32 * q, 32)
    for half in range(2):
        lanes = pl.ds(half * LANES, LANES)
        whole[pl.ds(0, 3 * KS), 0, lanes] = sums[half][: 3 * KS]
        whole[pl.ds(3 * KS + KL, 2), 0, lanes] = sums[half][3 * KS : 3 * KS + 2]
    leave(0, 3 * KS)
    leave(3 * KS + KL, 2)
    for copy in copies:
        copy.wait()


VMEM = pl.BlockSpec(memory_space=pltpu.VMEM)
HBM = pl.BlockSpec(memory_space=pltpu.HBM)


def call(kernel, name, outs, operands, scratch=(), ins=VMEM, in_hbm=None, flops=0):
    cost = pl.CostEstimate(flops=flops, bytes_accessed=0, transcendentals=0) if flops else None
    return pl.pallas_call(
        kernel,
        name=name,
        out_shape=[jax.ShapeDtypeStruct(shape, dtype) for shape, dtype in outs],
        in_specs=[ins] * len(operands),
        out_specs=[HBM if i == in_hbm else VMEM for i in range(len(outs))],
        scratch_shapes=[s if not isinstance(s, tuple) else pltpu.VMEM(*s) for s in scratch],
        cost_estimate=cost,
        compiler_params=pltpu.CompilerParams(vmem_limit_bytes=20 * 1024 * 1024),
    )(*operands)


def block(rows):
    return ((rows, SHARDS, LANES), f32)


def on_device(inputs, out_grad, short_filters, long_filters, skip_gain, norm_gain):
    chan = lax.axis_size("chan")
    width = chan * inputs.shape[2]
    params = ((PARAMS, LANES), f32)
    sums = ((2 * chan, 4, LANES), f32)
    wide = ((SHARDS * ROWS, LANES), f32)
    rows, longer, thrice, taps, part_rows = block(ROWS), block(ROWS + 8), block(200), block(TAPS), block(QUARTER + 8)
    splits = [((PARTS, 48, SHARDS, LANES), f32), ((PARTS, 16, SHARDS, LANES), f32)]
    kept = ((SHARDS * ROWS, LANES), bf16)
    shorts, longs = ((SHORT_ROWS, LANES), f32), ((32, LANES), f32)

    (packed,) = call(
        pack_kernel, "pack", [((SHARDS, 2 * ROWS, LANES), bf16)],
        tuple(pltpu.with_memory_space_constraint(a, pltpu.HBM) for a in (inputs, out_grad)),
        [((2, 2, ROWS, 2 * LANES), bf16), pltpu.SemaphoreType.DMA((2,))], HBM,
    )
    arrived = lax.all_to_all(packed, "seq", 0, 0)
    stored = (short_filters.transpose(1, 2, 0, 3), long_filters, skip_gain, norm_gain)
    own, send = call(
        halves_kernel, "halves", [params] * 2, tuple(pltpu.with_memory_space_constraint(a, pltpu.HBM) for a in stored),
        [(a.shape, f32) for a in stored] + [pltpu.SemaphoreType.DMA((4,))], HBM,
    )
    other = lax.ppermute(send, "section", [(0, 1), (1, 0)])
    taps0, token = call(spread_kernel, "spread", [taps, block(1)], (own, other))
    x0, g, part = call(open_kernel, "open", [rows, rows, sums], (arrived, token), [wide])

    def over_channels(part):
        return lax.all_to_all(part, ("section", "chan"), 0, 0)

    x1, q0, mixed0, normed0, f0, k0, v0, scaled0, part = call(
        functools.partial(first_kernel, width), "first",
        [kept, rows, kept] + [part_rows] * 4 + [block(QUARTER), sums], (x0, over_channels(part), taps0),
        [thrice, longer, rows, longer, longer, longer] + splits,
    )
    base, cubes, after1, mixed1, short1, part = call(
        functools.partial(second_kernel, width), "second",
        [rows, ((4, LANES), f32), kept, kept, shorts, sums], (x1, g, over_channels(part), own, other),
        [longer, thrice, thrice] + [longer] * 3 + [rows] * 6 + splits + [taps, sums, pltpu.SemaphoreType.DMA], in_hbm=5,
    )
    all_part = over_channels(part)
    long1, window0, taps0 = call(
        aside_kernel, "aside", [longs, block(112), taps], (after1, mixed1, mixed0, own, other), [block(112), rows],
        flops=2000000,
    )
    (message,) = call(
        third_kernel, "third", [((2 * SHARDS, MESSAGE, LANES), bf16)],
        (base, x1, cubes, all_part, taps0, window0, scaled0, normed0, mixed0, q0, f0, k0, v0, short1, long1),
        [block(216)] + [longer] * 4 + [((MESSAGE, LANES), f32)] + splits,
    )
    gathered = lax.all_to_all(message, ("section", "seq"), 0, 0)
    result = ((3 * KS + KL + 2, 1, 2 * LANES), f32)
    (grads,) = call(close_kernel, "close", [result], (gathered,), [result, pltpu.SemaphoreType.DMA((6,))], in_hbm=0)
    return grads.transpose(1, 0, 2)


def solution(mesh):
    placed = (
        P(None, "seq", "chan"),
        P(None, "seq", "chan"),
        P("section", None, None, "chan"),
        P("section", None, "chan"),
        P("section", "chan"),
        P("section", "chan"),
    )
    return jax.shard_map(
        on_device, mesh=mesh, in_specs=placed, out_specs=P("section", None, "chan"), check_vma=False
    )
```

profile of v0, /device:TPU:32, one launch (start us, length us, event | category | flops | bytes accessed | tf_op | source)
XLA Modules:
  0.0 82.8 jit_solution(15726562648326885166)
XLA Ops:
  0.0 1.6 %pack.1 = bf16[8,128,128]{2,1,0:T(8,128)(2,1)} custom-call(bf16[2,64,256]{2,1,0:T(8,128)(2,1)} %x_ref.1, bf16[2,64,256]{2,1,0:T(8,128)(2,1)} %g_ref.1), custom_call_target="tpu_custom_call" | custom-call | tf_op jit(solution)/shard_map/pack/pallas_call | solution.py:472
  1.6 8.6 %all-to-all-start = ((bf16[8,128,128]{2,1,0:T(8,128)(2,1)}), bf16[8,128,128]{2,1,0:T(8,128)(2,1)S(1)}, u32[]{:S(2)}, u32[]{:S(2)}) async-start(bf16[8,128,128]{2,1,0:T(8,128)(2,1)} %pack.1), calls=%async_computation | async-start | bytes 524288 | tf_op jit(solution)/shard_map/all_to_all | solution.py:504
  10.2 1.0 %halves.1 = (f32[152,128]{1,0:T(8,128)S(1)}, f32[152,128]{1,0:T(8,128)S(1)}) custom-call(f32[3,7,1,256]{3,2,1,0:T(1,128)} %bitcast.2, f32[1,128,256]{2,1,0:T(8,128)} %long_hbm.1, f32[1,256]{1,0:T(1,128)} %skip_hbm.1, f32[1,256]{1,0:T(1,128)} %gain_hbm.1), custom_call_target="tpu_custom_call" | custom-call | tf_op jit(solution)/shard_map/halves/pallas_call | solution.py:472
  11.2 0.1 collective-permute-start
  11.3 1.3 %collective-permute-done.other_ref = f32[152,128]{1,0:T(8,128)S(1)} collective-permute-done((f32[152,128]{1,0:T(8,128)S(1)}, f32[152,128]{1,0:T(8,128)S(1)}, u32[]{:S(2)}, u32[]{:S(2)}) %collective-permute-start) | collective-permute-done | bytes 77856 | tf_op jit(solution)/shard_map/ppermute | solution.py:510
  12.6 0.2 spread.1
  12.7 7.9 %all-to-all-done.in_ref = bf16[8,128,128]{2,1,0:T(8,128)(2,1)S(1)} async-done(((bf16[8,128,128]{2,1,0:T(8,128)(2,1)}), bf16[8,128,128]{2,1,0:T(8,128)(2,1)S(1)}, u32[]{:S(2)}, u32[]{:S(2)}) %all-to-all-start) | async-done | bytes 262176 | tf_op jit(solution)/shard_map/all_to_all | solution.py:504
  20.6 0.4 open.1
  21.1 14.6 %all_to_all.25.sums_ref = f32[32,4,128]{2,1,0:T(4,128)S(1)} all-to-all(f32[32,4,128]{2,1,0:T(4,128)S(1)} %get-tuple-element.34), channel_id=1, replica_groups=mesh['section'=2,'seq'=8,'chan'=16] {'section','chan'}, dimensions={0} | all-to-all | bytes 131072 | tf_op jit(solution)/shard_map/all_to_all | solution.py:515
  35.6 2.3 %first.1 = (bf16[512,128]{1,0:T(8,128)(2,1)S(1)}, f32[64,8,128]{2,1,0:T(8,128)S(1)}, bf16[512,128]{1,0:T(8,128)(2,1)S(1)}, f32[24,8,128]{2,1,0:T(8,128)S(1)}, f3...) custom-call(f32[64,8,128]{2,1,0:T(8,128)S(1)} %get-tuple-element.33., ...), custom_call_target="tpu_custom_call" | custom-call | tf_op jit(solution)/shard_map/first/pallas_call | solution.py:472
  37.9 10.8 %all_to_all.26.sums_ref = f32[32,4,128]{2,1,0:T(4,128)S(1)} all-to-all(f32[32,4,128]{2,1,0:T(4,128)S(1)} %get-tuple-element.38), channel_id=1, replica_groups=mesh['section'=2,'seq'=8,'chan'=16] {'section','chan'}, dimensions={0} | all-to-all | bytes 131072 | tf_op jit(solution)/shard_map/all_to_all | solution.py:515
  48.7 5.2 %second.1 = (f32[64,8,128]{2,1,0:T(8,128)S(1)}, f32[4,128]{1,0:T(4,128)S(1)}, bf16[512,128]{1,0:T(8,128)(2,1)S(1)}, bf16[512,128]{1,0:T(8,128)(2,1)S(1)}, f32[32,128]{1,0:T(8,128)S(1)}, /*index=5*/f32[32,4,128]{2,1,0:T(4,128)}) custom-call(bf16[512,128]{1,0:T(8,128)(2,1)S(1)} %get-tuple-element.36.x_ref.x1_ref, f32[64,8,128]{2,1,0:T(8,128)S(1)} %get-tuple-element.37.g_ref, ...), custom_call_target="tpu_custom_call" | custom-call | tf_op jit(solution)/shard_map/second/pallas_call | solution.py:472
  54.0 3.9 %all-to-all-start.3 = ((f32[32,4,128]{2,1,0:T(4,128)}), f32[32,4,128]{2,1,0:T(4,128)S(1)}, u32[]{:S(2)}, u32[]{:S(2)}) async-start(f32[32,4,128]{2,1,0:T(4,128)} %get-tuple-element.41), calls=%async_computation.3 | async-start | bytes 131072 | tf_op jit(solution)/shard_map/all_to_all | solution.py:515
  57.9 1.3 %aside.1 = (f32[32,128]{1,0:T(8,128)S(1)}, f32[112,8,128]{2,1,0:T(8,128)S(1)}, f32[312,8,128]{2,1,0:T(8,128)S(1)}) custom-call(bf16[512,128]{1,0:T(8,128)(2,1)S(1)} %get-tuple-element.42.after_ref, bf16[512,128]{1,0:T(8,128)(2,1)S(1)} %get-tuple-element.43.mixed1_ref, bf16[512,128]{1,0:T(8,128)(2,1)S(1)} %get-tuple-element.44.mixed0_ref.mixed_ref, ...), custom_call_target="tpu_custom_call" | custom-call | flops 2000000 | tf_op jit(solution)/shard_map/aside/pallas_call | solution.py:472
  59.2 6.1 %all-to-all-done.3.sums_ref = f32[32,4,128]{2,1,0:T(4,128)S(1)} async-done(((f32[32,4,128]{2,1,0:T(4,128)}), f32[32,4,128]{2,1,0:T(4,128)S(1)}, u32[]{:S(2)}, u32[]{:S(2)}) %all-to-all-start.3) | async-done | bytes 65568 | tf_op jit(solution)/shard_map/all_to_all | solution.py:515
  65.3 1.8 %third.1 = bf16[16,64,128]{2,1,0:T(8,128)(2,1)S(1)} custom-call(f32[64,8,128]{2,1,0:T(8,128)S(1)} %get-tuple-element.39.base_ref, bf16[512,128]{1,0:T(8,128)(2,1)S(1)} %get-tuple-element.36.x_ref.x1_ref, f32[4,128]{1,0:T(4,128)S(1)} %get-tuple-element.40.cubes_ref, f32[32,4,128]{2,1,0:T(4,128)S(1)} %all-to-all-done.3.sums_ref, ...), custom_call_target="tpu_custom_call" | custom-call | tf_op jit(solution)/shard_map/third/pallas_call | solution.py:472
  67.1 14.9 %all_to_all.27.in_ref = bf16[16,64,128]{2,1,0:T(8,128)(2,1)S(1)} all-to-all(bf16[16,64,128]{2,1,0:T(8,128)(2,1)S(1)} %third.1), channel_id=1, replica_groups=mesh['section'=2,'seq'=8,'chan'=16] {'section','seq'}, dimensions={0} | all-to-all | bytes 524288 | tf_op jit(solution)/shard_map/all_to_all | solution.py:537
  82.0 0.8 close.1
Async XLA Ops:
  1.6 19.0 %all-to-all-start = ((bf16[8,128,128]{2,1,0:T(8,128)(2,1)}), bf16[8,128,128]{2,1,0:T(8,128)(2,1)S(1)}, u32[]{:S(2)}, u32[]{:S(2)}) async-start(bf16[8,128,128]{2,1,0:T(8,128)(2,1)} %pack.1), calls=%async_computation | async-start | bytes 524288 | tf_op jit(solution)/shard_map/all_to_all | solution.py:504
  11.2 1.4 %collective-permute-start = (f32[152,128]{1,0:T(8,128)S(1)}, f32[152,128]{1,0:T(8,128)S(1)}, u32[]{:S(2)}, u32[]{:S(2)}) collective-permute-start(f32[152,128]{1,0:T(8,128)S(1)} %get-tuple-element.31), channel_id=1, source_target_pairs={{0,128},{128,0},{1,129},{129,1},{2,130},{130,2},{3,131},{131,3},{4... | collective-permute-start | bytes 233480 | tf_op jit(solution)/shard_map/ppermute | solution.py:510
  54.0 11.3 %all-to-all-start.3 = ((f32[32,4,128]{2,1,0:T(4,128)}), f32[32,4,128]{2,1,0:T(4,128)S(1)}, u32[]{:S(2)}, u32[]{:S(2)}) async-start(f32[32,4,128]{2,1,0:T(4,128)} %get-tuple-element.41), calls=%async_computation.3 | async-start | bytes 131072 | tf_op jit(solution)/shard_map/all_to_all | solution.py:515
where the time goes:
time: 83.2 us; the launch traced here: 82.8 us
  blocking collectives  40.3 us (48%)
  waiting for transfers between devices  15.3 us (18%)
  Pallas kernels  14.6 us (18%)
  starting transfers between devices  12.5 us (15%)
    all_to_all x2, blocking collectives, over_channels(): return lax.all_to_all(part, ('section', 'chan'), 0, 0)  25.4 us
    all_to_all x1, blocking collectives, on_device(): gathered = lax.all_to_all(message, ('section', 'seq'), 0, 0)  14.9 us
    pallas_call x9, Pallas kernels, call(): pl.pallas_call(kernel, name=name, out_shape=[jax.ShapeDtypeStruct(shape,...  14.6 us
    all_to_all x1, starting transfers between devices, on_device(): arrived = lax.all_to_all(packed, 'seq', 0, 0)  8.58 us
    all_to_all x1, waiting for transfers between devices, on_device(): arrived = lax.all_to_all(packed, 'seq', 0, 0)  7.91 us
    all_to_all x1, waiting for transfers between devices, over_channels(): return lax.all_to_all(part, ('section', 'chan'), 0, 0)  6.1 us
    all_to_all x1, starting transfers between devices, over_channels(): return lax.all_to_all(part, ('section', 'chan'), 0, 0)  3.87 us
  transfers between devices with their start and end apart: 3, of which 3 were waited for; matrix products, arithmetic and copies ran while one was open for 0% of the time, Pallas kernels for 3%

commit v1 on v0

--- a/solution.py
+++ b/solution.py
@@ -58,6 +58,14 @@
     return jnp.broadcast_to(column, (LANES, LANES)).reshape(16, SHARDS, LANES)
 
 
+def total_of(ref):
+    parts = ref[...]
+    while parts.shape[0] > 1:
+        half = parts.shape[0] // 2
+        parts = parts[:half] + parts[half:]
+    return parts[0]
+
+
 def sixteen_of(ref, b):
     if len(ref.shape) == 3:
         return ref[pl.ds(16 * b, 16)]
@@ -66,7 +74,7 @@
 
 
 def scale_and_norm(width, x_ref, sums_ref, taps, scale_ref, normed):
-    total = jnp.sum(sums_ref[...], axis=0)
+    total = total_of(sums_ref)
     scale_rows = lax.rsqrt(total * (1.0 / width) + EPSILON)
     diagonal = eye()
     gain = taps[GAIN_AT]
@@ -386,7 +394,9 @@
     copy.wait()
 
 
-def aside_kernel(after_ref, mixed1_ref, mixed0_ref, own_ref, other_ref, grads_ref, window0, taps, window1, after):
+def aside_kernel(
+    after_ref, mixed1_ref, mixed0_ref, own_ref, other_ref, short_ref, message_ref, window0, taps, window1, after, grads
+):
     q = lax.axis_index("seq") // 2
     window_before(mixed1_ref, q, window1)
 
@@ -394,17 +404,19 @@
     def _(b):
         after[pl.ds(b * 8, 8)] = rows_of(after_ref, b)
 
-    long_sums(grads_ref, 0, after, window1)
+    grads[pl.ds(0, SHORT_ROWS), :] = short_ref[...]
+    long_sums(grads, SHORT_ROWS, after, window1)
+    message_ref[...] = grads[...].astype(bf16)
     window_before(mixed0_ref, q, window0)
     spread(own_ref, other_ref, 0, taps)
 
 
 def third_kernel(
     base_ref, x1_ref, cubes_ref, sums_ref, taps, window, scaled_part, normed_part, mixed_ref, q_ref, f_part, k_part, v_part,
-    short1_ref, long1_ref, out_ref, after, errors, sq, sk, sv, grads, signals, results
+    message1_ref, out_ref, after, errors, sq, sk, sv, grads, signals, results
 ):
     q = lax.axis_index("seq") // 2
-    total = jnp.sum(sums_ref[...], axis=0) * cubes_ref[...]
+    total = total_of(sums_ref) * cubes_ref[...]
     diagonal = eye()
     for b in range(4):
         at = pl.ds(16 * b, 16)
@@ -431,7 +443,7 @@
     sums_of_rows(grads, (sq, sk, sv), start, normed_part[...], product, gain_term)
     long_sums(grads, SHORT_ROWS, after, window)
     message0 = grads[...].astype(bf16)
-    message1 = jnp.concatenate([short1_ref[...], long1_ref[...]], axis=0).astype(bf16)
+    message1 = message1_ref[...]
     for z in range(SHARDS):
         out_ref[z] = message0
         out_ref[SHARDS + z] = message1
@@ -494,7 +506,7 @@
     rows, longer, thrice, taps, part_rows = block(ROWS), block(ROWS + 8), block(200), block(TAPS), block(QUARTER + 8)
     splits = [((PARTS, 48, SHARDS, LANES), f32), ((PARTS, 16, SHARDS, LANES), f32)]
     kept = ((SHARDS * ROWS, LANES), bf16)
-    shorts, longs = ((SHORT_ROWS, LANES), f32), ((32, LANES), f32)
+    shorts = ((SHORT_ROWS, LANES), f32)
 
     (packed,) = call(
         pack_kernel, "pack", [((SHARDS, 2 * ROWS, LANES), bf16)],
@@ -525,13 +537,14 @@
         [longer, thrice, thrice] + [longer] * 3 + [rows] * 6 + splits + [taps, sums, pltpu.SemaphoreType.DMA], in_hbm=5,
     )
     all_part = over_channels(part)
-    long1, window0, taps0 = call(
-        aside_kernel, "aside", [longs, block(112), taps], (after1, mixed1, mixed0, own, other), [block(112), rows],
+    message1, window0, taps0 = call(
+        aside_kernel, "aside", [((MESSAGE, LANES), bf16), block(112), taps],
+        (after1, mixed1, mixed0, own, other, short1), [block(112), rows, ((MESSAGE, LANES), f32)],
         flops=2000000,
     )
     (message,) = call(
         third_kernel, "third", [((2 * SHARDS, MESSAGE, LANES), bf16)],
-        (base, x1, cubes, all_part, taps0, window0, scaled0, normed0, mixed0, q0, f0, k0, v0, short1, long1),
+        (base, x1, cubes, all_part, taps0, window0, scaled0, normed0, mixed0, q0, f0, k0, v0, message1),
         [block(216)] + [longer] * 4 + [((MESSAGE, LANES), f32)] + splits,
     )
     gathered = lax.all_to_all(message, ("section", "seq"), 0, 0)

time: 83.2 us -> 83.1 us (level)
  no operation moved by 1% of the time
where the time goes in v1:
time: 83.1 us; the launch traced here: 82.7 us
  blocking collectives  40.3 us (48%)
  waiting for transfers between devices  15.1 us (18%)
  Pallas kernels  14.6 us (18%)
  starting transfers between devices  12.5 us (15%)
    all_to_all x2, blocking collectives, over_channels(): return lax.all_to_all(part, ('section', 'chan'), 0, 0)  25.4 us
    all_to_all x1, blocking collectives, on_device(): gathered = lax.all_to_all(message, ('section', 'seq'), 0, 0)  14.9 us
    pallas_call x9, Pallas kernels, call(): pl.pallas_call(kernel, name=name, out_shape=[jax.ShapeDtypeStruct(shape,...  14.6 us
    all_to_all x1, starting transfers between devices, on_device(): arrived = lax.all_to_all(packed, 'seq', 0, 0)  8.58 us
    all_to_all x1, waiting for transfers between devices, on_device(): arrived = lax.all_to_all(packed, 'seq', 0, 0)  7.91 us
    all_to_all x1, waiting for transfers between devices, over_channels(): return lax.all_to_all(part, ('section', 'chan'), 0, 0)  5.97 us
    all_to_all x1, starting transfers between devices, over_channels(): return lax.all_to_all(part, ('section', 'chan'), 0, 0)  3.87 us
  transfers between devices with their start and end apart: 3, of which 3 were waited for; matrix products, arithmetic and copies ran while one was open for 0% of the time, Pallas kernels for 3%

profile of v1, /device:TPU:32, one launch (start us, length us, event | category | flops | bytes accessed | tf_op | source)
XLA Modules:
  0.0 82.7 jit_solution(1486173227601443529)
XLA Ops:
  0.0 1.6 %pack.1 = bf16[8,128,128]{2,1,0:T(8,128)(2,1)} custom-call(bf16[2,64,256]{2,1,0:T(8,128)(2,1)} %x_ref.1, bf16[2,64,256]{2,1,0:T(8,128)(2,1)} %g_ref.1), custom_call_target="tpu_custom_call" | custom-call | tf_op jit(solution)/shard_map/pack/pallas_call | solution.py:484
  1.6 8.6 %all-to-all-start = ((bf16[8,128,128]{2,1,0:T(8,128)(2,1)}), bf16[8,128,128]{2,1,0:T(8,128)(2,1)S(1)}, u32[]{:S(2)}, u32[]{:S(2)}) async-start(bf16[8,128,128]{2,1,0:T(8,128)(2,1)} %pack.1), calls=%async_computation | async-start | bytes 524288 | tf_op jit(solution)/shard_map/all_to_all | solution.py:516
  10.2 1.0 %halves.1 = (f32[152,128]{1,0:T(8,128)S(1)}, f32[152,128]{1,0:T(8,128)S(1)}) custom-call(f32[3,7,1,256]{3,2,1,0:T(1,128)} %bitcast.2, f32[1,128,256]{2,1,0:T(8,128)} %long_hbm.1, f32[1,256]{1,0:T(1,128)} %skip_hbm.1, f32[1,256]{1,0:T(1,128)} %gain_hbm.1), custom_call_target="tpu_custom_call" | custom-call | tf_op jit(solution)/shard_map/halves/pallas_call | solution.py:484
  11.2 0.1 collective-permute-start
  11.3 1.3 %collective-permute-done.other_ref = f32[152,128]{1,0:T(8,128)S(1)} collective-permute-done((f32[152,128]{1,0:T(8,128)S(1)}, f32[152,128]{1,0:T(8,128)S(1)}, u32[]{:S(2)}, u32[]{:S(2)}) %collective-permute-start) | collective-permute-done | bytes 77856 | tf_op jit(solution)/shard_map/ppermute | solution.py:522
  12.6 0.2 spread.1
  12.7 7.9 %all-to-all-done.in_ref = bf16[8,128,128]{2,1,0:T(8,128)(2,1)S(1)} async-done(((bf16[8,128,128]{2,1,0:T(8,128)(2,1)}), bf16[8,128,128]{2,1,0:T(8,128)(2,1)S(1)}, u32[]{:S(2)}, u32[]{:S(2)}) %all-to-all-start) | async-done | bytes 262176 | tf_op jit(solution)/shard_map/all_to_all | solution.py:516
  20.6 0.4 open.1
  21.1 14.6 %all_to_all.25.sums_ref = f32[32,4,128]{2,1,0:T(4,128)S(1)} all-to-all(f32[32,4,128]{2,1,0:T(4,128)S(1)} %get-tuple-element.34), channel_id=1, replica_groups=mesh['section'=2,'seq'=8,'chan'=16] {'section','chan'}, dimensions={0} | all-to-all | bytes 131072 | tf_op jit(solution)/shard_map/all_to_all | solution.py:527
  35.6 2.2 %first.1 = (bf16[512,128]{1,0:T(8,128)(2,1)S(1)}, f32[64,8,128]{2,1,0:T(8,128)S(1)}, bf16[512,128]{1,0:T(8,128)(2,1)S(1)}, f32[24,8,128]{2,1,0:T(8,128)S(1)}, f3...) custom-call(f32[64,8,128]{2,1,0:T(8,128)S(1)} %get-tuple-element.33., ...), custom_call_target="tpu_custom_call" | custom-call | tf_op jit(solution)/shard_map/first/pallas_call | solution.py:484
  37.9 10.8 %all_to_all.26.sums_ref = f32[32,4,128]{2,1,0:T(4,128)S(1)} all-to-all(f32[32,4,128]{2,1,0:T(4,128)S(1)} %get-tuple-element.38), channel_id=1, replica_groups=mesh['section'=2,'seq'=8,'chan'=16] {'section','chan'}, dimensions={0} | all-to-all | bytes 131072 | tf_op jit(solution)/shard_map/all_to_all | solution.py:527
  48.7 5.2 %second.1 = (f32[64,8,128]{2,1,0:T(8,128)S(1)}, f32[4,128]{1,0:T(4,128)S(1)}, bf16[512,128]{1,0:T(8,128)(2,1)S(1)}, bf16[512,128]{1,0:T(8,128)(2,1)S(1)}, f32[32,128]{1,0:T(8,128)S(1)}, /*index=5*/f32[32,4,128]{2,1,0:T(4,128)}) custom-call(bf16[512,128]{1,0:T(8,128)(2,1)S(1)} %get-tuple-element.36.x_ref.x1_ref, f32[64,8,128]{2,1,0:T(8,128)S(1)} %get-tuple-element.37.g_ref, ...), custom_call_target="tpu_custom_call" | custom-call | tf_op jit(solution)/shard_map/second/pallas_call | solution.py:484
  53.9 3.9 %all-to-all-start.3 = ((f32[32,4,128]{2,1,0:T(4,128)}), f32[32,4,128]{2,1,0:T(4,128)S(1)}, u32[]{:S(2)}, u32[]{:S(2)}) async-start(f32[32,4,128]{2,1,0:T(4,128)} %get-tuple-element.41), calls=%async_computation.3 | async-start | bytes 131072 | tf_op jit(solution)/shard_map/all_to_all | solution.py:527
  57.8 1.4 %aside.1 = (bf16[64,128]{1,0:T(8,128)(2,1)S(1)}, f32[112,8,128]{2,1,0:T(8,128)S(1)}, f32[312,8,128]{2,1,0:T(8,128)S(1)}) custom-call(bf16[512,128]{1,0:T(8,128)(2,1)S(1)} %get-tuple-element.42.after_ref, bf16[512,128]{1,0:T(8,128)(2,1)S(1)} %get-tuple-element.43.mixed1_ref, bf16[512,128]{1,0:T(8,128)(2,1)S(1)} %get-tuple-element.44.mixed0_ref.mixed_ref, ...), custom_call_target="tpu_custom_call" | custom-call | flops 2000000 | tf_op jit(solution)/shard_map/aside/pallas_call | solution.py:484
  59.3 6.0 %all-to-all-done.3.sums_ref = f32[32,4,128]{2,1,0:T(4,128)S(1)} async-done(((f32[32,4,128]{2,1,0:T(4,128)}), f32[32,4,128]{2,1,0:T(4,128)S(1)}, u32[]{:S(2)}, u32[]{:S(2)}) %all-to-all-start.3) | async-done | bytes 65568 | tf_op jit(solution)/shard_map/all_to_all | solution.py:527
  65.2 1.8 %third.1 = bf16[16,64,128]{2,1,0:T(8,128)(2,1)S(1)} custom-call(f32[64,8,128]{2,1,0:T(8,128)S(1)} %get-tuple-element.39.base_ref, bf16[512,128]{1,0:T(8,128)(2,1)S(1)} %get-tuple-element.36.x_ref.x1_ref, f32[4,128]{1,0:T(4,128)S(1)} %get-tuple-element.40.cubes_ref, f32[32,4,128]{2,1,0:T(4,128)S(1)} %all-to-all-done.3.sums_ref, ...), custom_call_target="tpu_custom_call" | custom-call | tf_op jit(solution)/shard_map/third/pallas_call | solution.py:484
  67.0 14.9 %all_to_all.27.in_ref = bf16[16,64,128]{2,1,0:T(8,128)(2,1)S(1)} all-to-all(bf16[16,64,128]{2,1,0:T(8,128)(2,1)S(1)} %third.1), channel_id=1, replica_groups=mesh['section'=2,'seq'=8,'chan'=16] {'section','seq'}, dimensions={0} | all-to-all | bytes 524288 | tf_op jit(solution)/shard_map/all_to_all | solution.py:550
  81.9 0.8 close.1
Async XLA Ops:
  1.6 19.0 %all-to-all-start = ((bf16[8,128,128]{2,1,0:T(8,128)(2,1)}), bf16[8,128,128]{2,1,0:T(8,128)(2,1)S(1)}, u32[]{:S(2)}, u32[]{:S(2)}) async-start(bf16[8,128,128]{2,1,0:T(8,128)(2,1)} %pack.1), calls=%async_computation | async-start | bytes 524288 | tf_op jit(solution)/shard_map/all_to_all | solution.py:516
  11.2 1.4 %collective-permute-start = (f32[152,128]{1,0:T(8,128)S(1)}, f32[152,128]{1,0:T(8,128)S(1)}, u32[]{:S(2)}, u32[]{:S(2)}) collective-permute-start(f32[152,128]{1,0:T(8,128)S(1)} %get-tuple-element.31), channel_id=1, source_target_pairs={{0,128},{128,0},{1,129},{129,1},{2,130},{130,2},{3,131},{131,3},{4... | collective-permute-start | bytes 233480 | tf_op jit(solution)/shard_map/ppermute | solution.py:522
  53.9 11.3 %all-to-all-start.3 = ((f32[32,4,128]{2,1,0:T(4,128)}), f32[32,4,128]{2,1,0:T(4,128)S(1)}, u32[]{:S(2)}, u32[]{:S(2)}) async-start(f32[32,4,128]{2,1,0:T(4,128)} %get-tuple-element.41), calls=%async_computation.3 | async-start | bytes 131072 | tf_op jit(solution)/shard_map/all_to_all | solution.py:527
